TPU v7x, 32 devices: a whole 2x2x4 slice. The times are simulated.
32 devices in a mesh: dp: 4 (over y, x), tensor: 8 (over z, core).
Axes of the slice: x: 2, y: 2, z: 4, core: 2. Of those that a mesh axis runs over, the one named last changes fastest.
Arguments:
- hidden: bfloat16 [512, 8192], P('dp', 'tensor')
- norm_gain: float32 [8192], P('tensor'), may hold values from 0.5 to 1.5
- head: bfloat16 [8192, 36864], P(None, ('dp', 'tensor'))
- targets: int32 [512], P('dp'), may hold values from 0 to 36863
- old_logprob: float32 [512], P('dp'), may hold values from -20 to -1
- lengths: int32 [4], P('dp'), may hold values from 1 to 128, as said below
Outputs:
- new_logprob: float32 [512], P('dp')
- log_ratio: float32 [512], P('dp')
Inputs may be any that keep to these rules, and one draw needn't show every extreme that they name: `lengths`: every length is at least 1 and at most 128; some sequence has 128 live tokens and some has 1.
All inputs are finite; a program needn't handle non-finite values.
Results may differ from a plain program's by a relative error of at most 0.00094.
Values may be sent and summed in bfloat16 or wider, within the bound.
No kernel may reach another device: no remote copies, remote signals or barrier semaphores. Data moves between devices by JAX's collectives and lax.ppermute only.
A program may use at most 128 MiB of HBM per device.

v0:
```python
import jax
import jax.numpy as jnp
from jax import lax
from jax.sharding import PartitionSpec as P

D = 8192


def joined(part, axis, combine):
    gathered = jax.tree.map(lambda a: lax.all_gather(a, axis), part)

    def take(source):
        return jax.tree.map(lambda a: lax.dynamic_index_in_dim(a, source, 0, False), gathered)

    return lax.fori_loop(
        1, lax.axis_size(axis), lambda source, state: combine(state, take(source)), take(0)
    )


def combine_stats(first, second):
    top = jnp.maximum(first[0], second[0])
    total = first[1] * jnp.exp(first[0] - top) + second[1] * jnp.exp(second[0] - top)
    return (top, total, first[2] + second[2])


def body(hidden, norm_gain, head, targets, old_logprob, lengths):
    tok_rows = hidden.shape[0]
    values = hidden.astype(jnp.float32)
    sum_sq = lax.psum(jnp.sum(values * values, axis=1), "tensor")
    scaled = lax.rsqrt(sum_sq / D + 1e-06)
    normed = (values * scaled[:, None] * norm_gain[None, :]).astype(jnp.bfloat16)
    vocab_cols = head.shape[1]
    rows, target_all = (
        lax.all_gather(normed, "dp", axis=0, tiled=True),
        lax.all_gather(targets, "dp", axis=0, tiled=True),
    )
    logits = jnp.dot(
        lax.all_gather(rows, "tensor", axis=1, tiled=True), head, preferred_element_type=jnp.float32
    )
    vocab_start = lax.axis_index(("dp", "tensor")) * vocab_cols
    block_top = jnp.max(logits, axis=1)
    block_total = jnp.sum(jnp.exp(logits - block_top[:, None]), axis=1)
    column = vocab_start + jnp.arange(vocab_cols, dtype=jnp.int32)
    hits = column[None, :] == target_all[:, None]
    block_pick = jnp.sum(jnp.where(hits, logits, jnp.float32(0.0)), axis=1)
    top, total, picked = joined(
        (block_top, block_total, block_pick), ("dp", "tensor"), combine_stats
    )
    offset = lax.axis_index("dp") * tok_rows
    top = lax.dynamic_slice_in_dim(top, offset, tok_rows, 0)
    total = lax.dynamic_slice_in_dim(total, offset, tok_rows, 0)
    picked = lax.dynamic_slice_in_dim(picked, offset, tok_rows, 0)
    seq_count = lengths.shape[0]
    position = jnp.arange(tok_rows // seq_count, dtype=jnp.int32)
    live = (position[None, :] < lengths[:, None]).reshape(-1).astype(jnp.float32)
    logprob = picked - top - jnp.log(total)
    return (live * logprob, live * (logprob - old_logprob))


def solution(mesh):
    in_specs = (
        P("dp", "tensor"),
        P("tensor"),
        P(None, ("dp", "tensor")),
        P("dp"),
        P("dp"),
        P("dp"),
    )
    out_specs = (P("dp"), P("dp"))
    return jax.shard_map(body, mesh=mesh, in_specs=in_specs, out_specs=out_specs, check_vma=False)
```

profile of v0, /device:TPU:0, one launch (start us, length us, event | category | flops | bytes accessed | tf_op | source)
XLA Modules:
  0.0 279.1 jit_solution(5263454632419754259)
XLA Ops:
  7.2 0.0 all-gather.10.cloned.1.call-start
  7.2 1.1 fusion
  8.3 18.1 %psum.7 = f32[128]{0:T(128)S(1)} all-reduce(f32[128]{0:T(128)S(1)} %fusion), channel_id=1, replica_groups=mesh['dp'=4,'tensor'=8] {'tensor'}, use_global_device_ids=true, to_apply=%region_1.0 | all-reduce | flops 128 | bytes 1024 | tf_op jit(solution)/shard_map/psum | solution.py:29
  26.4 1.8 fusion.2
  28.2 0.0 all-gather.10.cloned.1.call-update
  28.2 0.0 all-gather.12.cloned.1.call-start
  28.2 24.9 %all-gather.10.cloned.1.call-done = bf16[512,1024]{1,0:T(8,128)(2,1)} async-done(((bf16[128,1024]{1,0:T(8,128)(2,1)}), bf16[512,1024]{1,0:T(8,128)(2,1)}) %all-gather.10.cloned.1.call-update) | async-done | bytes 1048592 | tf_op jit(solution)/shard_map/all_gather | solution.py:34
  53.2 0.0 all-gather.12.cloned.1.call-update
  53.8 7.9 %all-gather.5 = s32[4,1,128]{2,1,0:T(1,128)S(1)} all-gather(s32[1,1,128]{2,1,0:T(1,128)} %bitcast.44), channel_id=1, replica_groups=mesh['dp'=4,'tensor'=8] {'dp'}, dimensions={0}, use_global_device_ids=true | all-gather | bytes 2560 | tf_op jit(solution)/shard_map/all_gather | solution.py:35
  61.7 75.2 %all-gather.12.cloned.1.call-done = bf16[512,8192]{1,0:T(8,128)(2,1)} async-done(((bf16[512,1024]{1,0:T(8,128)(2,1)}), bf16[512,8192]{1,0:T(8,128)(2,1)}) %all-gather.12.cloned.1.call-update) | async-done | bytes 8388624 | tf_op jit(solution)/shard_map/all_gather | solution.py:38
  136.9 16.3 %fusion.3 = (f32[512]{0:T(512)S(1)}, f32[512,1152]{1,0:T(8,128)S(1)}) fusion(bf16[512,8192]{1,0:T(8,128)(2,1)} %all-gather.12.cloned.1.call-done, bf16[8192,1152]{1,0:T(8,128)(2,1)} %param.10), kind=kOutput, calls=%fused_computation.19 | convolution fusion | flops 9664266240 | bytes 29624320 | tf_op jit(solution)/shard_map/dot_general | solution.py:37
  153.2 0.0 copy-start
  153.2 39.2 %all-gather.3 = f32[32,1,512]{2,1,0:T(1,128)S(1)} all-gather(f32[1,1,512]{2,1,0:T(1,128)S(1)} %bitcast.40), channel_id=2, replica_groups=mesh['dp'=4,'tensor'=8] {'dp','tensor'}, dimensions={0}, use_global_device_ids=true | all-gather | bytes 67584 | tf_op jit(solution)/shard_map/all_gather | solution.py:10
  192.4 0.7 select_reduce_fusion
  193.1 36.9 %all-gather.4 = f32[32,1,512]{2,1,0:T(1,128)S(1)} all-gather(f32[1,1,512]{2,1,0:T(1,128)S(1)} %bitcast.42), channel_id=3, replica_groups=mesh['dp'=4,'tensor'=8] {'dp','tensor'}, dimensions={0}, use_global_device_ids=true | all-gather | bytes 67584 | tf_op jit(solution)/shard_map/all_gather | solution.py:10
  230.0 38.2 %all-gather.6 = f32[32,1,512]{2,1,0:T(1,128)S(1)} all-gather(f32[1,1,512]{2,1,0:T(1,128)S(1)} %bitcast.41), channel_id=4, replica_groups=mesh['dp'=4,'tensor'=8] {'dp','tensor'}, dimensions={0}, use_global_device_ids=true | all-gather | bytes 67584 | tf_op jit(solution)/shard_map/all_gather | solution.py:10
  268.3 2.9 %while.19 = (s32[]{:T(128)}, f32[512]{0:T(512)S(1)}, f32[512]{0:T(512)S(1)}, f32[512]{0:T(512)S(1)}, f32[32,512]{1,0:T(8,128)S(1)}, /*index=5*/f32[32,512]{1,0:T...) while((s32[]{:T(128)}, f32[512]{0:T(512)S(1)}, f32[512]{0:T(512)S(1)}, f32[512]{0:T(512)S(1)}, ...), condition=%wide.region_6.7_spmd, body=%wide.region_5.6_spmd.sunk | while | flops 3589 | bytes 30871 | solution.py:15
  271.1 0.0 copy-done
  271.1 0.6 compare_select_fusion
  271.7 0.5 compare_select_fusion.1
  (132 shorter events, 1.7 us)
Async XLA Ops:
  7.2 46.0 %all-gather.10.cloned.1.call-start = ((), (), s32[]{:S(2)}) async-start(), calls=%async_computation | async-start | bytes 1310720 | tf_op jit(solution)/shard_map/all_gather | solution.py:34
  28.2 108.7 %all-gather.12.cloned.1.call-start = ((), (), s32[]{:S(2)}) async-start(), calls=%async_computation.1 | async-start | bytes 9437184 | tf_op jit(solution)/shard_map/all_gather | solution.py:38
  153.2 118.0 %copy-start = (f32[128]{0:T(128)S(1)}, f32[128]{0:T(128)}, u32[]{:S(2)}) copy-start(f32[128]{0:T(128)} %param.12) | copy-start | bytes 1540
Sparse Core Ops, SparseCore 0:
  28.3 24.8 all-gather.9
  54.8 82.0 all-gather.11
where the time goes:
time: 279 us
  blocking collectives  140 us (50%)
  waiting for transfers between devices  100 us (36%)
  matrix products  16.3 us (6%)
  between operations  14.7 us (5%)
  other arithmetic  5.63 us (2%)
    all_gather x3, blocking collectives, joined(): gathered = jax.tree.map(lambda a: lax.all_gather(a, axis), part)  114 us
    all_gather x1, waiting for transfers between devices, body(): lax.all_gather(rows, 'tensor', axis=1, tiled=True)  75.2 us
    all_gather x1, waiting for transfers between devices, body(): lax.all_gather(normed, 'dp', axis=0, tiled=True)  24.9 us
    psum x1, blocking collectives, body(): sum_sq = lax.psum(jnp.sum(values * values, axis=1), 'tensor')  18.1 us
    dot_general x1, matrix products, body(): jnp.dot(lax.all_gather(rows, 'tensor', axis=1, tiled=True), head, preferr...  16.3 us
    all_gather x1, blocking collectives, body(): lax.all_gather(targets, 'dp', axis=0, tiled=True)  7.86 us
  transfers between devices with their start and end apart: 2, of which 2 were waited for; matrix products, arithmetic and copies ran while one was open for 0% of the time, Pallas kernels for 0%

commit v1 on v0

v1 whole, which is shorter than its diff:
```python
import jax
import jax.numpy as jnp
from jax import lax
from jax.sharding import PartitionSpec as P

D = 8192
CORES = 2


def sender(n_dp, n_t):
    cols = 2
    rows = n_dp // cols
    depth = n_t // CORES

    def send(a, dy=0, dx=0, dz=0, dc=0):
        perm = []
        for y in range(rows):
            for x in range(cols):
                for z in range(depth):
                    for c in range(CORES):
                        src = (y * cols + x) * n_t + z * CORES + c
                        dst = ((y + dy) % rows * cols + (x + dx) % cols) * n_t
                        dst += (z + dz) % depth * CORES + (c + dc) % CORES
                        perm.append((src, dst))
        return lax.ppermute(a, ("dp", "tensor"), perm)

    return rows, cols, depth, send


def body(hidden, norm_gain, head, targets, old_logprob, lengths):
    n_dp, n_t = lax.axis_size("dp"), lax.axis_size("tensor")
    rows, cols, depth, send = sender(n_dp, n_t)
    tok, feat = hidden.shape
    half = tok // 2
    tensor = lax.axis_index("tensor")
    z_me, c_me = tensor // CORES, tensor % CORES
    plane = [(dy, dx) for dy in range(rows) for dx in range(cols)]
    others = [(dz, dc) for dz in range(depth) for dc in range(CORES)]

    values = hidden.astype(jnp.float32)
    own_sq = jnp.sum(values * values, axis=1)
    packed = jnp.concatenate([norm_gain, own_sq])
    fine = {o: send(packed, dz=o[0], dc=o[1]) if any(o) else packed for o in others}
    layers = [hidden] + [send(hidden, dz=dz) for dz in range(1, depth)]

    sum_sq = sum(fine[o][feat:] for o in others)
    scaled = lax.rsqrt(sum_sq / D + 1e-06)
    marks = jnp.concatenate([scaled, targets.astype(jnp.float32)])
    coarse = {p: send(marks, dy=p[0], dx=p[1]) if any(p) else marks for p in plane}
    scale_all = jnp.concatenate([coarse[p][:tok] for p in plane])
    target_all = jnp.concatenate([coarse[p][tok:] for p in plane]).astype(jnp.int32)

    vocab_cols = head.shape[1]
    logits = jnp.zeros((tok * n_dp, vocab_cols), jnp.float32)
    for dz, mine in enumerate(layers):
        got = {(0, 0): mine}
        for dx in range(1, cols):
            got[0, dx] = send(mine, dx=dx)
        for dy in range(1, rows):
            got[dy, 0] = send(mine, dy=dy)
        for dy in range(1, rows):
            for dx in range(1, cols):
                first = send(got[0, dx][:half], dy=dy)
                second = send(got[dy, 0][half:], dx=dx)
                got[dy, dx] = jnp.concatenate([first, second])
        block = jnp.concatenate([got[p] for p in plane])
        sibling = send(block, dc=1)
        for dc, part in ((0, block), (1, sibling)):
            gain = fine[dz, dc][:feat]
            normed = (part.astype(jnp.float32) * scale_all[:, None] * gain[None, :]).astype(jnp.bfloat16)
            source = (z_me - dz) % depth * CORES + (c_me - dc) % CORES
            weights = lax.dynamic_slice_in_dim(head, source * feat, feat, 0)
            logits = logits + jnp.dot(normed, weights, preferred_element_type=jnp.float32)

    vocab_start = lax.axis_index(("dp", "tensor")) * vocab_cols
    block_top = jnp.max(logits, axis=1)
    block_total = jnp.sum(jnp.exp(logits - block_top[:, None]), axis=1)
    column = vocab_start + jnp.arange(vocab_cols, dtype=jnp.int32)
    hits = column[None, :] == target_all[:, None]
    block_pick = jnp.sum(jnp.where(hits, logits, jnp.float32(0.0)), axis=1)
    stats = jnp.stack([block_top, block_total, block_pick])

    def merge(parts):
        top = parts[0][0]
        for p in parts[1:]:
            top = jnp.maximum(top, p[0])
        total = sum(p[1] * jnp.exp(p[0] - top) for p in parts)
        return jnp.stack([top, total, sum(p[2] for p in parts)])

    pieces = {p: stats[:, i * tok : (i + 1) * tok] for i, p in enumerate(plane)}
    stats = merge([send(pieces[p], dy=-p[0], dx=-p[1]) if any(p) else pieces[p] for p in plane])
    stats = merge([send(stats, dz=o[0], dc=o[1]) if any(o) else stats for o in others])
    top, total, picked = stats[0], stats[1], stats[2]

    seq_count = lengths.shape[0]
    position = jnp.arange(tok // seq_count, dtype=jnp.int32)
    live = (position[None, :] < lengths[:, None]).reshape(-1).astype(jnp.float32)
    logprob = picked - top - jnp.log(total)
    return (live * logprob, live * (logprob - old_logprob))


def solution(mesh):
    in_specs = (
        P("dp", "tensor"),
        P("tensor"),
        P(None, ("dp", "tensor")),
        P("dp"),
        P("dp"),
        P("dp"),
    )
    out_specs = (P("dp"), P("dp"))
    return jax.shard_map(body, mesh=mesh, in_specs=in_specs, out_specs=out_specs, check_vma=False)
```

time: 279 us -> 105 us (0.38)
  blocking collectives: 140 us -> 0 us
  waiting for transfers between devices: 100 us -> 26.6 us
  starting transfers between devices: 0.08 us -> 50.3 us
  between operations: 14.7 us -> 2.01 us
  matrix products: 16.3 us -> 20.1 us
    all_gather x4 -> x0, blocking collectives: 122 us -> none  [the longest x3 114 us: joined(): gathered = jax.tree.map(lambda a: lax.all_gather(a, axis), part)]
    all_gather x2 -> x0, waiting for transfers between devices: 100 us -> none  [the longest x1 75.2 us: body(): lax.all_gather(rows, 'tensor', axis=1, tiled=True)]
    ppermute x0 -> x43, starting transfers between devices: none -> 50.3 us  [send(): return lax.ppermute(a, ('dp', 'tensor'), perm)]
    ppermute x0 -> x43, waiting for transfers between devices: none -> 26.6 us  [send(): return lax.ppermute(a, ('dp', 'tensor'), perm)]
    psum x1 -> x0, blocking collectives: 18.1 us -> none  [body(): sum_sq = lax.psum(jnp.sum(values * values, axis=1), 'tensor')]
    dot_general x1 -> x8, matrix products: 16.3 us -> 20.1 us  [body(): jnp.dot(normed, weights, preferred_element_type=jnp.float32)]
  transfers between devices with their start and end apart: 2 -> 43, of which waited for: 2 -> 17; matrix products, arithmetic and copies ran while one was open for 0% -> 19% of each run, Pallas kernels for 0% -> 0%
where the time goes in v1:
time: 105 us
  starting transfers between devices  50.3 us (48%)
  waiting for transfers between devices  26.6 us (25%)
  matrix products  20.1 us (19%)
  other arithmetic  4.28 us (4%)
  between operations  2.01 us (2%)
  local copies, waits for them, and re-layouts  1.44 us (1%)
    ppermute x43, starting transfers between devices, send(): return lax.ppermute(a, ('dp', 'tensor'), perm)  50.3 us
    ppermute x43, waiting for transfers between devices, send(): return lax.ppermute(a, ('dp', 'tensor'), perm)  26.6 us
    dot_general x8, matrix products, body(): jnp.dot(normed, weights, preferred_element_type=jnp.float32)  20.1 us
  transfers between devices with their start and end apart: 43, of which 17 were waited for; matrix products, arithmetic and copies ran while one was open for 19% of the time, Pallas kernels for 0%

profile of v1, /device:TPU:0, one launch (start us, length us, event | category | flops | bytes accessed | tf_op | source)
XLA Modules:
  0.0 104.7 jit_solution(13991707781742180849)
XLA Ops:
  0.6 1.1 %multiply_reduce_fusion = f32[128]{0:T(128)S(1)} fusion(bf16[128,1024]{1,0:T(8,128)(2,1)} %param.6), kind=kLoop, calls=%fused_computation.42 | loop fusion | flops 393088 | bytes 262656 | tf_op jit(solution)/shard_map/reduce_sum | solution.py:41
  2.9 2.6 %collective-permute-start.1 = (f32[1152]{0:T(1024)S(1)}, f32[1152]{0:T(1024)S(1)}, u32[]{:S(2)}, u32[]{:S(2)}) collective-permute-start(f32[1152]{0:T(1024)S(1)} %pad_maximum_fusion), channel_id=1, source_target_pairs={{0,2},{1,3},{2,4},{3,5},{4,6},{5,7},{6,0},{7,1},{8,10},{9,11},{10,... | collective-permute-start | bytes 13832 | tf_op jit(solution)/shard_map/ppermute | solution.py:25
  5.4 1.4 %collective-permute-start.2 = (f32[1152]{0:T(1024)S(1)}, f32[1152]{0:T(1024)S(1)}, u32[]{:S(2)}, u32[]{:S(2)}) collective-permute-start(f32[1152]{0:T(1024)S(1)} %pad_maximum_fusion), channel_id=1, source_target_pairs={{0,3},{1,2},{2,5},{3,4},{4,7},{5,6},{6,1},{7,0},{8,11},{9,10},{10,... | collective-permute-start | bytes 13832 | tf_op jit(solution)/shard_map/ppermute | solution.py:25
  6.9 1.3 %collective-permute-start.3 = (f32[1152]{0:T(1024)S(1)}, f32[1152]{0:T(1024)S(1)}, u32[]{:S(2)}, u32[]{:S(2)}) collective-permute-start(f32[1152]{0:T(1024)S(1)} %pad_maximum_fusion), channel_id=1, source_target_pairs={{0,4},{1,5},{2,6},{3,7},{4,0},{5,1},{6,2},{7,3},{8,12},{9,13},{10,... | collective-permute-start | bytes 13832 | tf_op jit(solution)/shard_map/ppermute | solution.py:25
  8.2 1.2 %collective-permute-start.4 = (f32[1152]{0:T(1024)S(1)}, f32[1152]{0:T(1024)S(1)}, u32[]{:S(2)}, u32[]{:S(2)}) collective-permute-start(f32[1152]{0:T(1024)S(1)} %pad_maximum_fusion), channel_id=1, source_target_pairs={{0,5},{1,4},{2,7},{3,6},{4,1},{5,0},{6,3},{7,2},{8,13},{9,12},{10,... | collective-permute-start | bytes 13832 | tf_op jit(solution)/shard_map/ppermute | solution.py:25
  9.4 1.0 constant_dynamic-update-slice_fusion.4
  10.4 2.3 %collective-permute-start.5 = (f32[1152]{0:T(1024)S(1)}, f32[1152]{0:T(1024)S(1)}, u32[]{:S(2)}, u32[]{:S(2)}) collective-permute-start(f32[1152]{0:T(1024)S(1)} %pad_maximum_fusion), channel_id=1, source_target_pairs={{0,6},{1,7},{2,0},{3,1},{4,2},{5,3},{6,4},{7,5},{8,14},{9,15},{10,... | collective-permute-start | bytes 13832 | tf_op jit(solution)/shard_map/ppermute | solution.py:25
  13.8 1.5 %collective-permute-start.10 = (bf16[128,1024]{1,0:T(8,128)(2,1)}, bf16[128,1024]{1,0:T(8,128)(2,1)S(1)}, u32[]{:S(2)}, u32[]{:S(2)}) collective-permute-start(bf16[128,1024]{1,0:T(8,128)(2,1)} %param.6), channel_id=1, source_target_pairs={{0,8},{1,9},{2,10},{3,11},{4,12},{5,13},{6,14},{7,15},{8,0},{9,1},... | collective-permute-start | bytes 786440 | tf_op jit(solution)/shard_map/ppermute | solution.py:25
  15.3 1.5 %collective-permute-start.11 = (bf16[128,1024]{1,0:T(8,128)(2,1)}, bf16[128,1024]{1,0:T(8,128)(2,1)S(1)}, u32[]{:S(2)}, u32[]{:S(2)}) collective-permute-start(bf16[128,1024]{1,0:T(8,128)(2,1)} %param.6), channel_id=1, source_target_pairs={{0,16},{1,17},{2,18},{3,19},{4,20},{5,21},{6,22},{7,23},{8,24},{9,... | collective-permute-start | bytes 786440 | tf_op jit(solution)/shard_map/ppermute | solution.py:25
  16.8 1.5 %collective-permute-start.15 = (bf16[128,1024]{1,0:T(8,128)(2,1)}, bf16[128,1024]{1,0:T(8,128)(2,1)S(1)}, u32[]{:S(2)}, u32[]{:S(2)}) collective-permute-start(bf16[128,1024]{1,0:T(8,128)(2,1)} %param.6), channel_id=1, source_target_pairs={{0,2},{1,3},{2,4},{3,5},{4,6},{5,7},{6,0},{7,1},{8,10},{9,11},{10,... | collective-permute-start | bytes 786440 | tf_op jit(solution)/shard_map/ppermute | solution.py:25
  19.7 3.0 %collective-permute-done.7 = f32[256]{0:T(256)S(1)} collective-permute-done((f32[256]{0:T(256)S(1)}, f32[256]{0:T(256)S(1)}, u32[]{:S(2)}, u32[]{:S(2)}) %collective-permute-start.7) | collective-permute-done | bytes 1056 | tf_op jit(solution)/shard_map/ppermute | solution.py:25
  22.8 1.2 %collective-permute-start.8 = (f32[256]{0:T(256)S(1)}, f32[256]{0:T(256)S(1)}, u32[]{:S(2)}, u32[]{:S(2)}) collective-permute-start(f32[256]{0:T(256)S(1)} %pad_maximum_fusion.7), channel_id=1, source_target_pairs={{0,16},{1,17},{2,18},{3,19},{4,20},{5,21},{6,22},{7,23},{8,24},{9,... | collective-permute-start | bytes 3080 | tf_op jit(solution)/shard_map/ppermute | solution.py:25
  24.0 2.3 %collective-permute-done.8 = f32[256]{0:T(256)S(1)} collective-permute-done((f32[256]{0:T(256)S(1)}, f32[256]{0:T(256)S(1)}, u32[]{:S(2)}, u32[]{:S(2)}) %collective-permute-start.8) | collective-permute-done | bytes 1056 | tf_op jit(solution)/shard_map/ppermute | solution.py:25
  26.3 2.1 %collective-permute-start.9 = (f32[256]{0:T(256)S(1)}, f32[256]{0:T(256)S(1)}, u32[]{:S(2)}, u32[]{:S(2)}) collective-permute-start(f32[256]{0:T(256)S(1)} %pad_maximum_fusion.7), channel_id=1, source_target_pairs={{0,24},{1,25},{2,26},{3,27},{4,28},{5,29},{6,30},{7,31},{8,16},{9,... | collective-permute-start | bytes 3080 | tf_op jit(solution)/shard_map/ppermute | solution.py:25
  28.5 2.3 %collective-permute-done.9 = f32[256]{0:T(256)S(1)} collective-permute-done((f32[256]{0:T(256)S(1)}, f32[256]{0:T(256)S(1)}, u32[]{:S(2)}, u32[]{:S(2)}) %collective-permute-start.9) | collective-permute-done | bytes 1056 | tf_op jit(solution)/shard_map/ppermute | solution.py:25
  30.8 1.7 %collective-permute-start.27 = (bf16[128,1024]{1,0:T(8,128)(2,1)}, bf16[128,1024]{1,0:T(8,128)(2,1)S(1)}, u32[]{:S(2)}, u32[]{:S(2)}) collective-permute-start(bf16[128,1024]{1,0:T(8,128)(2,1)} %param.6), channel_id=1, source_target_pairs={{0,6},{1,7},{2,0},{3,1},{4,2},{5,3},{6,4},{7,5},{8,14},{9,15},{10,... | collective-permute-start | bytes 786440 | tf_op jit(solution)/shard_map/ppermute | solution.py:25
  32.5 1.4 %collective-permute-start.12 = (bf16[64,1024]{1,0:T(8,128)(2,1)S(1)}, bf16[64,1024]{1,0:T(8,128)(2,1)S(1)}, u32[]{:S(2)}, u32[]{:S(2)}) collective-permute-start(bf16[64,1024]{1,0:T(8,128)(2,1)S(1)} %slice.281), channel_id=1, source_target_pairs={{0,16},{1,17},{2,18},{3,19},{4,20},{5,21},{6,22},{7,23},{8,24},{9,... | collective-permute-start | bytes 393224 | tf_op jit(solution)/shard_map/ppermute | solution.py:25
  34.0 1.6 %collective-permute-start.13 = (bf16[64,1024]{1,0:T(8,128)(2,1)S(1)}, bf16[64,1024]{1,0:T(8,128)(2,1)S(1)}, u32[]{:S(2)}, u32[]{:S(2)}) collective-permute-start(bf16[64,1024]{1,0:T(8,128)(2,1)S(1)} %slice.282), channel_id=1, source_target_pairs={{0,8},{1,9},{2,10},{3,11},{4,12},{5,13},{6,14},{7,15},{8,0},{9,1},... | collective-permute-start | bytes 393224 | tf_op jit(solution)/shard_map/ppermute | solution.py:25
  36.1 1.9 %collective-permute-done.21 = bf16[128,1024]{1,0:T(8,128)(2,1)S(1)} collective-permute-done((bf16[128,1024]{1,0:T(8,128)(2,1)}, bf16[128,1024]{1,0:T(8,128)(2,1)S(1)}, u32[]{:S(2)}, u32[]{:S(2)}) %collective-permute-start.21) | collective-permute-done | bytes 262176 | tf_op jit(solution)/shard_map/ppermute | solution.py:25
  38.6 3.4 %collective-permute-done.27 = bf16[128,1024]{1,0:T(8,128)(2,1)S(1)} collective-permute-done((bf16[128,1024]{1,0:T(8,128)(2,1)}, bf16[128,1024]{1,0:T(8,128)(2,1)S(1)}, u32[]{:S(2)}, u32[]{:S(2)}) %collective-permute-start.27) | collective-permute-done | bytes 262176 | tf_op jit(solution)/shard_map/ppermute | solution.py:25
  42.0 1.5 %collective-permute-start.22 = (bf16[128,1024]{1,0:T(8,128)(2,1)S(1)}, bf16[128,1024]{1,0:T(8,128)(2,1)S(1)}, u32[]{:S(2)}, u32[]{:S(2)}) collective-permute-start(bf16[128,1024]{1,0:T(8,128)(2,1)S(1)} %collective-permute-done.21), channel_id=1, source_target_pairs={{0,8},{1,9},{2,10},{3,11},{4,12},{5,13},{6,14},{7,15},{8,0},{9,1},... | collective-permute-start | bytes 786440 | tf_op jit(solution)/shard_map/ppermute | solution.py:25
  43.5 1.0 collective-permute-start.23
  44.6 1.2 %collective-permute-start.28 = (bf16[128,1024]{1,0:T(8,128)(2,1)S(1)}, bf16[128,1024]{1,0:T(8,128)(2,1)S(1)}, u32[]{:S(2)}, u32[]{:S(2)}) collective-permute-start(bf16[128,1024]{1,0:T(8,128)(2,1)S(1)} %collective-permute-done.27), channel_id=1, source_target_pairs={{0,8},{1,9},{2,10},{3,11},{4,12},{5,13},{6,14},{7,15},{8,0},{9,1},... | collective-permute-start | bytes 786440 | tf_op jit(solution)/shard_map/ppermute | solution.py:25
  45.8 3.4 %fusion.7 = f32[512,1152]{1,0:T(8,128)S(1)} fusion(bf16[8192,1152]{1,0:T(8,128)(2,1)} %param.8, s32[]{:T(128)S(6)} %select_n.87, bf16[512,1024]{1,0:T(8,128)(2,1)S(1)} %constant_dynamic-update-slice_fusion, f32[1024]{0:T(1024)S(1)} %copy-done, f32[512]{0:T(512)S(1)} %pad_maximum_fusion.5), kind=kOutput, calls=%fused_computation.16 | convolution fusion | flops 1210056704 | bytes 5773316 | tf_op jit(solution)/shard_map/dot_general | solution.py:73
  50.0 1.3 %collective-permute-done.22 = bf16[128,1024]{1,0:T(8,128)(2,1)S(1)} collective-permute-done((bf16[128,1024]{1,0:T(8,128)(2,1)S(1)}, bf16[128,1024]{1,0:T(8,128)(2,1)S(1)}, u32[]{:S(2)}, u32[]{:S(2)}) %collective-permute-start.22) | collective-permute-done | bytes 262176 | tf_op jit(solution)/shard_map/ppermute | solution.py:25
  51.2 1.5 %collective-permute-start.18 = (bf16[64,1024]{1,0:T(8,128)(2,1)S(1)}, bf16[64,1024]{1,0:T(8,128)(2,1)S(1)}, u32[]{:S(2)}, u32[]{:S(2)}) collective-permute-start(bf16[64,1024]{1,0:T(8,128)(2,1)S(1)} %slice.284), channel_id=1, source_target_pairs={{0,16},{1,17},{2,18},{3,19},{4,20},{5,21},{6,22},{7,23},{8,24},{9,... | collective-permute-start | bytes 393224 | tf_op jit(solution)/shard_map/ppermute | solution.py:25
  52.8 0.9 collective-permute-start.19
  53.8 1.6 %collective-permute-done.28 = bf16[128,1024]{1,0:T(8,128)(2,1)S(1)} collective-permute-done((bf16[128,1024]{1,0:T(8,128)(2,1)S(1)}, bf16[128,1024]{1,0:T(8,128)(2,1)S(1)}, u32[]{:S(2)}, u32[]{:S(2)}) %collective-permute-start.28) | collective-permute-done | bytes 262176 | tf_op jit(solution)/shard_map/ppermute | solution.py:25
  55.4 2.8 %collective-permute-start.24 = (bf16[64,1024]{1,0:T(8,128)(2,1)S(1)}, bf16[64,1024]{1,0:T(8,128)(2,1)S(1)}, u32[]{:S(2)}, u32[]{:S(2)}) collective-permute-start(bf16[64,1024]{1,0:T(8,128)(2,1)S(1)} %slice.288), channel_id=1, source_target_pairs={{0,16},{1,17},{2,18},{3,19},{4,20},{5,21},{6,22},{7,23},{8,24},{9,... | collective-permute-start | bytes 393224 | tf_op jit(solution)/shard_map/ppermute | solution.py:25
  58.6 0.9 collective-permute-start.25
  59.5 1.8 %collective-permute-done.18 = bf16[64,1024]{1,0:T(8,128)(2,1)S(1)} collective-permute-done((bf16[64,1024]{1,0:T(8,128)(2,1)S(1)}, bf16[64,1024]{1,0:T(8,128)(2,1)S(1)}, u32[]{:S(2)}, u32[]{:S(2)}) %collective-permute-start.18) | collective-permute-done | bytes 131104 | tf_op jit(solution)/shard_map/ppermute | solution.py:25
  62.8 1.3 %collective-permute-done.24 = bf16[64,1024]{1,0:T(8,128)(2,1)S(1)} collective-permute-done((bf16[64,1024]{1,0:T(8,128)(2,1)S(1)}, bf16[64,1024]{1,0:T(8,128)(2,1)S(1)}, u32[]{:S(2)}, u32[]{:S(2)}) %collective-permute-start.24) | collective-permute-done | bytes 131104 | tf_op jit(solution)/shard_map/ppermute | solution.py:25
  65.0 1.4 %collective-permute-done.30 = bf16[64,1024]{1,0:T(8,128)(2,1)S(1)} collective-permute-done((bf16[64,1024]{1,0:T(8,128)(2,1)S(1)}, bf16[64,1024]{1,0:T(8,128)(2,1)S(1)}, u32[]{:S(2)}, u32[]{:S(2)}) %collective-permute-start.30) | collective-permute-done | bytes 131104 | tf_op jit(solution)/shard_map/ppermute | solution.py:25
  67.4 3.4 %convolution_add_fusion.6 = f32[512,1152]{1,0:T(8,128)S(1)} fusion(f32[512,1152]{1,0:T(8,128)S(1)} %fusion.7, bf16[8192,1152]{1,0:T(8,128)(2,1)} %param.8, s32[]{:T(128)S(6)} %select_n.89, bf16[512,1024]{1,0:T(8,128)(2,1)S(1)} %collective-permute-done.14, f32[1024]{0:T(1024)S(1)} %slice-done.6, f32[512]{0:T(512)S(1)} %pad_maximum_fusion.5), kind=kOutput, calls=%fused_computation.6 | convolution fusion | flops 1210646528 | bytes 8132612 | tf_op jit(solution)/shard_map/dot_general | solution.py:73
  70.8 3.4 %convolution_add_fusion.5 = f32[512,1152]{1,0:T(8,128)S(1)} fusion(f32[512,1152]{1,0:T(8,128)S(1)} %convolution_add_fusion.6, bf16[8192,1152]{1,0:T(8,128)(2,1)} %param.8, s32[]{:T(128)S(6)} %select_n.91, bf16[512,1024]{1,0:T(8,128)(2,1)S(1)} %constant_dynamic-update-slice_fusion.5, f32[1024]{0:T(1024)S(1)} %slice-done.5, f32[512]{0:T(512)S(1)} %pad_maximum_fusion.5), kind=kOutput, calls=%fused_computation.5 | convolution fusion | flops 1210646528 | bytes 8132612 | tf_op jit(solution)/shard_map/dot_general | solution.py:73
  74.3 3.4 %convolution_add_fusion.4 = f32[512,1152]{1,0:T(8,128)S(1)} fusion(f32[512,1152]{1,0:T(8,128)S(1)} %convolution_add_fusion.5, bf16[8192,1152]{1,0:T(8,128)(2,1)} %param.8, s32[]{:T(128)S(6)} %select_n.92, bf16[512,1024]{1,0:T(8,128)(2,1)S(1)} %collective-permute-done.20, f32[1024]{0:T(1024)S(1)} %slice-done.4, f32[512]{0:T(512)S(1)} %pad_maximum_fusion.5), kind=kOutput, calls=%fused_computation.4 | convolution fusion | flops 1210646528 | bytes 8132612 | tf_op jit(solution)/shard_map/dot_general | solution.py:73
  77.8 1.6 %convolution_add_fusion.3 = f32[512,1152]{1,0:T(8,128)S(1)} fusion(f32[512,1152]{1,0:T(8,128)S(1)} %convolution_add_fusion.4, bf16[8192,1152]{1,0:T(8,128)(2,1)S(1)} %bitcast.225, s32[]{:T(128)S(6)} %select_n.94, bf16[512,1024]{1,0:T(8,128)(2,1)S(1)} %constant_dynamic-update-slice_fusion.10, f32[1024]{0:T(1024)S(1)} %slice-done.3, f32[512]{0:T(512)S(1)} %pad_maximum_fusion.5), kind=kOutput, calls=%fused_computation.3 | convolution fusion | flops 1210646528 | bytes 8132612 | tf_op jit(solution)/shard_map/dot_general | solution.py:73
  79.4 1.6 %convolution_add_fusion.2 = f32[512,1152]{1,0:T(8,128)S(1)} fusion(f32[512,1152]{1,0:T(8,128)S(1)} %convolution_add_fusion.3, bf16[8192,1152]{1,0:T(8,128)(2,1)S(1)} %bitcast.225, s32[]{:T(128)S(6)} %select_n.95, bf16[512,1024]{1,0:T(8,128)(2,1)S(1)} %collective-permute-done.26, f32[1024]{0:T(1024)S(1)} %slice-done.2, f32[512]{0:T(512)S(1)} %pad_maximum_fusion.5), kind=kOutput, calls=%fused_computation.2 | convolution fusion | flops 1210646528 | bytes 8132612 | tf_op jit(solution)/shard_map/dot_general | solution.py:73
  81.0 1.6 %convolution_add_fusion.1 = f32[512,1152]{1,0:T(8,128)S(1)} fusion(f32[512,1152]{1,0:T(8,128)S(1)} %convolution_add_fusion.2, bf16[8192,1152]{1,0:T(8,128)(2,1)S(1)} %bitcast.225, s32[]{:T(128)S(6)} %select_n.97, bf16[512,1024]{1,0:T(8,128)(2,1)S(1)} %constant_dynamic-update-slice_fusion.15, f32[1024]{0:T(1024)S(1)} %slice-done.1, f32[512]{0:T(512)S(1)} %pad_maximum_fusion.5), kind=kOutput, calls=%fused_computation.1 | convolution fusion | flops 1210646528 | bytes 8132612 | tf_op jit(solution)/shard_map/dot_general | solution.py:73
  82.6 1.7 %fusion.64 = (f32[512]{0:T(512)S(1)}, f32[512,1152]{1,0:T(8,128)S(1)}) fusion(f32[512,1152]{1,0:T(8,128)S(1)} %convolution_add_fusion.1, bf16[8192,1152]{1,0:T(8,128)(2,1)S(1)} %bitcast.225, s32[]{:T(128)S(6)} %select_n.98, bf16[512,1024]{1,0:T(8,128)(2,1)S(1)} %collective-permute-done.32, f32[1024]{0:T(1024)S(1)} %slice-done, f32[512]{0:T(512)S(1)} %pad_maximum_fusion.5), kind=kOutput, calls=%fused_computation.157 | convolution fusion | flops 1211235840 | bytes 8134660 | tf_op jit(solution)/shard_map/dot_general | solution.py:73
  85.6 1.6 %collective-permute-start.34 = (f32[3,128]{1,0:T(4,128)S(1)}, f32[3,128]{1,0:T(4,128)S(1)}, u32[]{:S(2)}, u32[]{:S(2)}) collective-permute-start(f32[3,128]{1,0:T(4,128)S(1)} %get-tuple-element.10), channel_id=1, source_target_pairs={{0,16},{1,17},{2,18},{3,19},{4,20},{5,21},{6,22},{7,23},{8,24},{9,... | collective-permute-start | bytes 4616 | tf_op jit(solution)/shard_map/ppermute | solution.py:25
  87.2 1.3 %collective-permute-start.35 = (f32[3,128]{1,0:T(4,128)S(1)}, f32[3,128]{1,0:T(4,128)S(1)}, u32[]{:S(2)}, u32[]{:S(2)}) collective-permute-start(f32[3,128]{1,0:T(4,128)S(1)} %get-tuple-element.11), channel_id=1, source_target_pairs={{0,24},{1,25},{2,26},{3,27},{4,28},{5,29},{6,30},{7,31},{8,16},{9,... | collective-permute-start | bytes 4616 | tf_op jit(solution)/shard_map/ppermute | solution.py:25
  89.2 2.5 %collective-permute-done.35 = f32[3,128]{1,0:T(4,128)S(1)} collective-permute-done((f32[3,128]{1,0:T(4,128)S(1)}, f32[3,128]{1,0:T(4,128)S(1)}, u32[]{:S(2)}, u32[]{:S(2)}) %collective-permute-start.35) | collective-permute-done | bytes 1568 | tf_op jit(solution)/shard_map/ppermute | solution.py:25
  91.8 1.9 %collective-permute-start.37 = (f32[3,128]{1,0:T(4,128)S(1)}, f32[3,128]{1,0:T(4,128)S(1)}, u32[]{:S(2)}, u32[]{:S(2)}) collective-permute-start(f32[3,128]{1,0:T(4,128)S(1)} %pad_maximum_fusion.6), channel_id=1, source_target_pairs={{0,2},{1,3},{2,4},{3,5},{4,6},{5,7},{6,0},{7,1},{8,10},{9,11},{10,... | collective-permute-start | bytes 4616 | tf_op jit(solution)/shard_map/ppermute | solution.py:25
  93.8 4.2 %collective-permute-start.39 = (f32[3,128]{1,0:T(4,128)S(1)}, f32[3,128]{1,0:T(4,128)S(1)}, u32[]{:S(2)}, u32[]{:S(2)}) collective-permute-start(f32[3,128]{1,0:T(4,128)S(1)} %pad_maximum_fusion.6), channel_id=1, source_target_pairs={{0,4},{1,5},{2,6},{3,7},{4,0},{5,1},{6,2},{7,3},{8,12},{9,13},{10,... | collective-permute-start | bytes 4616 | tf_op jit(solution)/shard_map/ppermute | solution.py:25
  98.0 2.6 %collective-permute-start.41 = (f32[3,128]{1,0:T(4,128)S(1)}, f32[3,128]{1,0:T(4,128)S(1)}, u32[]{:S(2)}, u32[]{:S(2)}) collective-permute-start(f32[3,128]{1,0:T(4,128)S(1)} %pad_maximum_fusion.6), channel_id=1, source_target_pairs={{0,6},{1,7},{2,0},{3,1},{4,2},{5,3},{6,4},{7,5},{8,14},{9,15},{10,... | collective-permute-start | bytes 4616 | tf_op jit(solution)/shard_map/ppermute | solution.py:25
  100.6 1.2 %collective-permute-start.42 = (f32[3,128]{1,0:T(4,128)S(1)}, f32[3,128]{1,0:T(4,128)S(1)}, u32[]{:S(2)}, u32[]{:S(2)}) collective-permute-start(f32[3,128]{1,0:T(4,128)S(1)} %pad_maximum_fusion.6), channel_id=1, source_target_pairs={{0,7},{1,6},{2,1},{3,0},{4,3},{5,2},{6,5},{7,4},{8,15},{9,14},{10,... | collective-permute-start | bytes 4616 | tf_op jit(solution)/shard_map/ppermute | solution.py:25
  102.5 1.1 %collective-permute-done.42 = f32[3,128]{1,0:T(4,128)S(1)} collective-permute-done((f32[3,128]{1,0:T(4,128)S(1)}, f32[3,128]{1,0:T(4,128)S(1)}, u32[]{:S(2)}, u32[]{:S(2)}) %collective-permute-start.42) | collective-permute-done | bytes 1568 | tf_op jit(solution)/shard_map/ppermute | solution.py:25
  (134 shorter events, 12.6 us)
Async XLA Ops:
  0.6 45.1 %copy-start = (f32[1024]{0:T(1024)S(1)}, f32[1024]{0:T(1024)}, u32[]{:S(2)}) copy-start(f32[1024]{0:T(1024)} %param.7) | copy-start | bytes 12292
  2.4 8.0 %collective-permute-start = (f32[1152]{0:T(1024)S(1)}, f32[1152]{0:T(1024)S(1)}, u32[]{:S(2)}, u32[]{:S(2)}) collective-permute-start(f32[1152]{0:T(1024)S(1)} %pad_maximum_fusion), channel_id=1, source_target_pairs={{0,1},{1,0},{2,3},{3,2},{4,5},{5,4},{6,7},{7,6},{8,9},{9,8},{10,11... | collective-permute-start | bytes 13832 | tf_op jit(solution)/shard_map/ppermute | solution.py:25
  2.9 9.9 %collective-permute-start.1 = (f32[1152]{0:T(1024)S(1)}, f32[1152]{0:T(1024)S(1)}, u32[]{:S(2)}, u32[]{:S(2)}) collective-permute-start(f32[1152]{0:T(1024)S(1)} %pad_maximum_fusion), channel_id=1, source_target_pairs={{0,2},{1,3},{2,4},{3,5},{4,6},{5,7},{6,0},{7,1},{8,10},{9,11},{10,... | collective-permute-start | bytes 13832 | tf_op jit(solution)/shard_map/ppermute | solution.py:25
  5.4 8.4 %collective-permute-start.2 = (f32[1152]{0:T(1024)S(1)}, f32[1152]{0:T(1024)S(1)}, u32[]{:S(2)}, u32[]{:S(2)}) collective-permute-start(f32[1152]{0:T(1024)S(1)} %pad_maximum_fusion), channel_id=1, source_target_pairs={{0,3},{1,2},{2,5},{3,4},{4,7},{5,6},{6,1},{7,0},{8,11},{9,10},{10,... | collective-permute-start | bytes 13832 | tf_op jit(solution)/shard_map/ppermute | solution.py:25
  6.9 8.4 %collective-permute-start.3 = (f32[1152]{0:T(1024)S(1)}, f32[1152]{0:T(1024)S(1)}, u32[]{:S(2)}, u32[]{:S(2)}) collective-permute-start(f32[1152]{0:T(1024)S(1)} %pad_maximum_fusion), channel_id=1, source_target_pairs={{0,4},{1,5},{2,6},{3,7},{4,0},{5,1},{6,2},{7,3},{8,12},{9,13},{10,... | collective-permute-start | bytes 13832 | tf_op jit(solution)/shard_map/ppermute | solution.py:25
  8.2 8.6 %collective-permute-start.4 = (f32[1152]{0:T(1024)S(1)}, f32[1152]{0:T(1024)S(1)}, u32[]{:S(2)}, u32[]{:S(2)}) collective-permute-start(f32[1152]{0:T(1024)S(1)} %pad_maximum_fusion), channel_id=1, source_target_pairs={{0,5},{1,4},{2,7},{3,6},{4,1},{5,0},{6,3},{7,2},{8,13},{9,12},{10,... | collective-permute-start | bytes 13832 | tf_op jit(solution)/shard_map/ppermute | solution.py:25
  10.4 38.7 %copy-start.7 = (f32[1152]{0:T(1024)}, f32[1152]{0:T(1024)S(1)}, u32[]{:S(2)}) copy-start(f32[1152]{0:T(1024)S(1)} %collective-permute-done) | copy-start | bytes 13828
  10.4 7.9 %collective-permute-start.5 = (f32[1152]{0:T(1024)S(1)}, f32[1152]{0:T(1024)S(1)}, u32[]{:S(2)}, u32[]{:S(2)}) collective-permute-start(f32[1152]{0:T(1024)S(1)} %pad_maximum_fusion), channel_id=1, source_target_pairs={{0,6},{1,7},{2,0},{3,1},{4,2},{5,3},{6,4},{7,5},{8,14},{9,15},{10,... | collective-permute-start | bytes 13832 | tf_op jit(solution)/shard_map/ppermute | solution.py:25
  12.8 36.4 %copy-start.6 = (f32[1152]{0:T(1024)}, f32[1152]{0:T(1024)S(1)}, u32[]{:S(2)}) copy-start(f32[1152]{0:T(1024)S(1)} %collective-permute-done.1) | copy-start | bytes 13828
  12.8 6.3 %collective-permute-start.6 = (f32[1152]{0:T(1024)S(1)}, f32[1152]{0:T(1024)S(1)}, u32[]{:S(2)}, u32[]{:S(2)}) collective-permute-start(f32[1152]{0:T(1024)S(1)} %pad_maximum_fusion), channel_id=1, source_target_pairs={{0,7},{1,6},{2,1},{3,0},{4,3},{5,2},{6,5},{7,4},{8,15},{9,14},{10,... | collective-permute-start | bytes 13832 | tf_op jit(solution)/shard_map/ppermute | solution.py:25
  13.8 35.4 %copy-start.5 = (f32[1152]{0:T(1024)}, f32[1152]{0:T(1024)S(1)}, u32[]{:S(2)}) copy-start(f32[1152]{0:T(1024)S(1)} %collective-permute-done.2) | copy-start | bytes 13828
  13.8 18.7 %collective-permute-start.10 = (bf16[128,1024]{1,0:T(8,128)(2,1)}, bf16[128,1024]{1,0:T(8,128)(2,1)S(1)}, u32[]{:S(2)}, u32[]{:S(2)}) collective-permute-start(bf16[128,1024]{1,0:T(8,128)(2,1)} %param.6), channel_id=1, source_target_pairs={{0,8},{1,9},{2,10},{3,11},{4,12},{5,13},{6,14},{7,15},{8,0},{9,1},... | collective-permute-start | bytes 786440 | tf_op jit(solution)/shard_map/ppermute | solution.py:25
  15.3 18.7 %collective-permute-start.11 = (bf16[128,1024]{1,0:T(8,128)(2,1)}, bf16[128,1024]{1,0:T(8,128)(2,1)S(1)}, u32[]{:S(2)}, u32[]{:S(2)}) collective-permute-start(bf16[128,1024]{1,0:T(8,128)(2,1)} %param.6), channel_id=1, source_target_pairs={{0,16},{1,17},{2,18},{3,19},{4,20},{5,21},{6,22},{7,23},{8,24},{9,... | collective-permute-start | bytes 786440 | tf_op jit(solution)/shard_map/ppermute | solution.py:25
  16.8 18.7 %collective-permute-start.15 = (bf16[128,1024]{1,0:T(8,128)(2,1)}, bf16[128,1024]{1,0:T(8,128)(2,1)S(1)}, u32[]{:S(2)}, u32[]{:S(2)}) collective-permute-start(bf16[128,1024]{1,0:T(8,128)(2,1)} %param.6), channel_id=1, source_target_pairs={{0,2},{1,3},{2,4},{3,5},{4,6},{5,7},{6,0},{7,1},{8,10},{9,11},{10,... | collective-permute-start | bytes 786440 | tf_op jit(solution)/shard_map/ppermute | solution.py:25
  18.3 19.7 %collective-permute-start.21 = (bf16[128,1024]{1,0:T(8,128)(2,1)}, bf16[128,1024]{1,0:T(8,128)(2,1)S(1)}, u32[]{:S(2)}, u32[]{:S(2)}) collective-permute-start(bf16[128,1024]{1,0:T(8,128)(2,1)} %param.6), channel_id=1, source_target_pairs={{0,4},{1,5},{2,6},{3,7},{4,0},{5,1},{6,2},{7,3},{8,12},{9,13},{10,... | collective-permute-start | bytes 786440 | tf_op jit(solution)/shard_map/ppermute | solution.py:25
  19.1 3.6 %collective-permute-start.7 = (f32[256]{0:T(256)S(1)}, f32[256]{0:T(256)S(1)}, u32[]{:S(2)}, u32[]{:S(2)}) collective-permute-start(f32[256]{0:T(256)S(1)} %pad_maximum_fusion.7), channel_id=1, source_target_pairs={{0,8},{1,9},{2,10},{3,11},{4,12},{5,13},{6,14},{7,15},{8,0},{9,1},... | collective-permute-start | bytes 3080 | tf_op jit(solution)/shard_map/ppermute | solution.py:25
  22.8 3.6 %collective-permute-start.8 = (f32[256]{0:T(256)S(1)}, f32[256]{0:T(256)S(1)}, u32[]{:S(2)}, u32[]{:S(2)}) collective-permute-start(f32[256]{0:T(256)S(1)} %pad_maximum_fusion.7), channel_id=1, source_target_pairs={{0,16},{1,17},{2,18},{3,19},{4,20},{5,21},{6,22},{7,23},{8,24},{9,... | collective-permute-start | bytes 3080 | tf_op jit(solution)/shard_map/ppermute | solution.py:25
  26.3 4.5 %collective-permute-start.9 = (f32[256]{0:T(256)S(1)}, f32[256]{0:T(256)S(1)}, u32[]{:S(2)}, u32[]{:S(2)}) collective-permute-start(f32[256]{0:T(256)S(1)} %pad_maximum_fusion.7), channel_id=1, source_target_pairs={{0,24},{1,25},{2,26},{3,27},{4,28},{5,29},{6,30},{7,31},{8,16},{9,... | collective-permute-start | bytes 3080 | tf_op jit(solution)/shard_map/ppermute | solution.py:25
  30.8 11.2 %collective-permute-start.27 = (bf16[128,1024]{1,0:T(8,128)(2,1)}, bf16[128,1024]{1,0:T(8,128)(2,1)S(1)}, u32[]{:S(2)}, u32[]{:S(2)}) collective-permute-start(bf16[128,1024]{1,0:T(8,128)(2,1)} %param.6), channel_id=1, source_target_pairs={{0,6},{1,7},{2,0},{3,1},{4,2},{5,3},{6,4},{7,5},{8,14},{9,15},{10,... | collective-permute-start | bytes 786440 | tf_op jit(solution)/shard_map/ppermute | solution.py:25
  32.5 11.0 %collective-permute-start.12 = (bf16[64,1024]{1,0:T(8,128)(2,1)S(1)}, bf16[64,1024]{1,0:T(8,128)(2,1)S(1)}, u32[]{:S(2)}, u32[]{:S(2)}) collective-permute-start(bf16[64,1024]{1,0:T(8,128)(2,1)S(1)} %slice.281), channel_id=1, source_target_pairs={{0,16},{1,17},{2,18},{3,19},{4,20},{5,21},{6,22},{7,23},{8,24},{9,... | collective-permute-start | bytes 393224 | tf_op jit(solution)/shard_map/ppermute | solution.py:25
  34.0 10.6 %collective-permute-start.13 = (bf16[64,1024]{1,0:T(8,128)(2,1)S(1)}, bf16[64,1024]{1,0:T(8,128)(2,1)S(1)}, u32[]{:S(2)}, u32[]{:S(2)}) collective-permute-start(bf16[64,1024]{1,0:T(8,128)(2,1)S(1)} %slice.282), channel_id=1, source_target_pairs={{0,8},{1,9},{2,10},{3,11},{4,12},{5,13},{6,14},{7,15},{8,0},{9,1},... | collective-permute-start | bytes 393224 | tf_op jit(solution)/shard_map/ppermute | solution.py:25
  35.5 13.7 %collective-permute-start.16 = (bf16[128,1024]{1,0:T(8,128)(2,1)S(1)}, bf16[128,1024]{1,0:T(8,128)(2,1)S(1)}, u32[]{:S(2)}, u32[]{:S(2)}) collective-permute-start(bf16[128,1024]{1,0:T(8,128)(2,1)S(1)} %collective-permute-done.15), channel_id=1, source_target_pairs={{0,8},{1,9},{2,10},{3,11},{4,12},{5,13},{6,14},{7,15},{8,0},{9,1},... | collective-permute-start | bytes 786440 | tf_op jit(solution)/shard_map/ppermute | solution.py:25
  38.0 11.8 %collective-permute-start.17 = (bf16[128,1024]{1,0:T(8,128)(2,1)S(1)}, bf16[128,1024]{1,0:T(8,128)(2,1)S(1)}, u32[]{:S(2)}, u32[]{:S(2)}) collective-permute-start(bf16[128,1024]{1,0:T(8,128)(2,1)S(1)} %collective-permute-done.15), channel_id=1, source_target_pairs={{0,16},{1,17},{2,18},{3,19},{4,20},{5,21},{6,22},{7,23},{8,24},{9,... | collective-permute-start | bytes 786440 | tf_op jit(solution)/shard_map/ppermute | solution.py:25
  42.0 9.2 %collective-permute-start.22 = (bf16[128,1024]{1,0:T(8,128)(2,1)S(1)}, bf16[128,1024]{1,0:T(8,128)(2,1)S(1)}, u32[]{:S(2)}, u32[]{:S(2)}) collective-permute-start(bf16[128,1024]{1,0:T(8,128)(2,1)S(1)} %collective-permute-done.21), channel_id=1, source_target_pairs={{0,8},{1,9},{2,10},{3,11},{4,12},{5,13},{6,14},{7,15},{8,0},{9,1},... | collective-permute-start | bytes 786440 | tf_op jit(solution)/shard_map/ppermute | solution.py:25
  43.5 34.2 %slice-start.7 = ((s8[18874368]{0:T(1024)(128)(4,1)}), s8[4194304]{0:T(1024)(128)(4,1)S(1)}, s32[]{:S(2)}) async-start(s8[18874368]{0:T(1024)(128)(4,1)} %bitcast.224), calls=%async_computation.7 | async-start | bytes 8388608
  43.5 9.3 %collective-permute-start.23 = (bf16[128,1024]{1,0:T(8,128)(2,1)S(1)}, bf16[128,1024]{1,0:T(8,128)(2,1)S(1)}, u32[]{:S(2)}, u32[]{:S(2)}) collective-permute-start(bf16[128,1024]{1,0:T(8,128)(2,1)S(1)} %collective-permute-done.21), channel_id=1, source_target_pairs={{0,16},{1,17},{2,18},{3,19},{4,20},{5,21},{6,22},{7,23},{8,24},{9,... | collective-permute-start | bytes 786440 | tf_op jit(solution)/shard_map/ppermute | solution.py:25
  44.6 10.8 %collective-permute-start.28 = (bf16[128,1024]{1,0:T(8,128)(2,1)S(1)}, bf16[128,1024]{1,0:T(8,128)(2,1)S(1)}, u32[]{:S(2)}, u32[]{:S(2)}) collective-permute-start(bf16[128,1024]{1,0:T(8,128)(2,1)S(1)} %collective-permute-done.27), channel_id=1, source_target_pairs={{0,8},{1,9},{2,10},{3,11},{4,12},{5,13},{6,14},{7,15},{8,0},{9,1},... | collective-permute-start | bytes 786440 | tf_op jit(solution)/shard_map/ppermute | solution.py:25
  49.2 9.3 %collective-permute-start.29 = (bf16[128,1024]{1,0:T(8,128)(2,1)S(1)}, bf16[128,1024]{1,0:T(8,128)(2,1)S(1)}, u32[]{:S(2)}, u32[]{:S(2)}) collective-permute-start(bf16[128,1024]{1,0:T(8,128)(2,1)S(1)} %collective-permute-done.27), channel_id=1, source_target_pairs={{0,16},{1,17},{2,18},{3,19},{4,20},{5,21},{6,22},{7,23},{8,24},{9,... | collective-permute-start | bytes 786440 | tf_op jit(solution)/shard_map/ppermute | solution.py:25
  49.8 17.5 %collective-permute-start.14 = (bf16[512,1024]{1,0:T(8,128)(2,1)S(1)}, bf16[512,1024]{1,0:T(8,128)(2,1)S(1)}, u32[]{:S(2)}, u32[]{:S(2)}) collective-permute-start(bf16[512,1024]{1,0:T(8,128)(2,1)S(1)} %constant_dynamic-update-slice_fusion), channel_id=1, source_target_pairs={{0,1},{1,0},{2,3},{3,2},{4,5},{5,4},{6,7},{7,6},{8,9},{9,8},{10,11... | collective-permute-start | bytes 3145736 | tf_op jit(solution)/shard_map/ppermute | solution.py:25
  51.2 10.1 %collective-permute-start.18 = (bf16[64,1024]{1,0:T(8,128)(2,1)S(1)}, bf16[64,1024]{1,0:T(8,128)(2,1)S(1)}, u32[]{:S(2)}, u32[]{:S(2)}) collective-permute-start(bf16[64,1024]{1,0:T(8,128)(2,1)S(1)} %slice.284), channel_id=1, source_target_pairs={{0,16},{1,17},{2,18},{3,19},{4,20},{5,21},{6,22},{7,23},{8,24},{9,... | collective-permute-start | bytes 393224 | tf_op jit(solution)/shard_map/ppermute | solution.py:25
  52.8 9.4 %collective-permute-start.19 = (bf16[64,1024]{1,0:T(8,128)(2,1)S(1)}, bf16[64,1024]{1,0:T(8,128)(2,1)S(1)}, u32[]{:S(2)}, u32[]{:S(2)}) collective-permute-start(bf16[64,1024]{1,0:T(8,128)(2,1)S(1)} %slice.285), channel_id=1, source_target_pairs={{0,8},{1,9},{2,10},{3,11},{4,12},{5,13},{6,14},{7,15},{8,0},{9,1},... | collective-permute-start | bytes 393224 | tf_op jit(solution)/shard_map/ppermute | solution.py:25
  55.4 8.8 %collective-permute-start.24 = (bf16[64,1024]{1,0:T(8,128)(2,1)S(1)}, bf16[64,1024]{1,0:T(8,128)(2,1)S(1)}, u32[]{:S(2)}, u32[]{:S(2)}) collective-permute-start(bf16[64,1024]{1,0:T(8,128)(2,1)S(1)} %slice.288), channel_id=1, source_target_pairs={{0,16},{1,17},{2,18},{3,19},{4,20},{5,21},{6,22},{7,23},{8,24},{9,... | collective-permute-start | bytes 393224 | tf_op jit(solution)/shard_map/ppermute | solution.py:25
  58.6 6.3 %collective-permute-start.25 = (bf16[64,1024]{1,0:T(8,128)(2,1)S(1)}, bf16[64,1024]{1,0:T(8,128)(2,1)S(1)}, u32[]{:S(2)}, u32[]{:S(2)}) collective-permute-start(bf16[64,1024]{1,0:T(8,128)(2,1)S(1)} %slice.289), channel_id=1, source_target_pairs={{0,8},{1,9},{2,10},{3,11},{4,12},{5,13},{6,14},{7,15},{8,0},{9,1},... | collective-permute-start | bytes 393224 | tf_op jit(solution)/shard_map/ppermute | solution.py:25
  61.4 5.0 %collective-permute-start.30 = (bf16[64,1024]{1,0:T(8,128)(2,1)S(1)}, bf16[64,1024]{1,0:T(8,128)(2,1)S(1)}, u32[]{:S(2)}, u32[]{:S(2)}) collective-permute-start(bf16[64,1024]{1,0:T(8,128)(2,1)S(1)} %slice.292), channel_id=1, source_target_pairs={{0,16},{1,17},{2,18},{3,19},{4,20},{5,21},{6,22},{7,23},{8,24},{9,... | collective-permute-start | bytes 393224 | tf_op jit(solution)/shard_map/ppermute | solution.py:25
  62.2 5.0 %collective-permute-start.31 = (bf16[64,1024]{1,0:T(8,128)(2,1)S(1)}, bf16[64,1024]{1,0:T(8,128)(2,1)S(1)}, u32[]{:S(2)}, u32[]{:S(2)}) collective-permute-start(bf16[64,1024]{1,0:T(8,128)(2,1)S(1)} %slice.293), channel_id=1, source_target_pairs={{0,8},{1,9},{2,10},{3,11},{4,12},{5,13},{6,14},{7,15},{8,0},{9,1},... | collective-permute-start | bytes 393224 | tf_op jit(solution)/shard_map/ppermute | solution.py:25
  64.2 10.1 %collective-permute-start.20 = (bf16[512,1024]{1,0:T(8,128)(2,1)S(1)}, bf16[512,1024]{1,0:T(8,128)(2,1)S(1)}, u32[]{:S(2)}, u32[]{:S(2)}) collective-permute-start(bf16[512,1024]{1,0:T(8,128)(2,1)S(1)} %constant_dynamic-update-slice_fusion.5), channel_id=1, source_target_pairs={{0,1},{1,0},{2,3},{3,2},{4,5},{5,4},{6,7},{7,6},{8,9},{9,8},{10,11... | collective-permute-start | bytes 3145736 | tf_op jit(solution)/shard_map/ppermute | solution.py:25
  64.9 14.5 %collective-permute-start.26 = (bf16[512,1024]{1,0:T(8,128)(2,1)S(1)}, bf16[512,1024]{1,0:T(8,128)(2,1)S(1)}, u32[]{:S(2)}, u32[]{:S(2)}) collective-permute-start(bf16[512,1024]{1,0:T(8,128)(2,1)S(1)} %constant_dynamic-update-slice_fusion.10), channel_id=1, source_target_pairs={{0,1},{1,0},{2,3},{3,2},{4,5},{5,4},{6,7},{7,6},{8,9},{9,8},{10,11... | collective-permute-start | bytes 3145736 | tf_op jit(solution)/shard_map/ppermute | solution.py:25
  67.3 15.3 %collective-permute-start.32 = (bf16[512,1024]{1,0:T(8,128)(2,1)S(1)}, bf16[512,1024]{1,0:T(8,128)(2,1)S(1)}, u32[]{:S(2)}, u32[]{:S(2)}) collective-permute-start(bf16[512,1024]{1,0:T(8,128)(2,1)S(1)} %constant_dynamic-update-slice_fusion.15), channel_id=1, source_target_pairs={{0,1},{1,0},{2,3},{3,2},{4,5},{5,4},{6,7},{7,6},{8,9},{9,8},{10,11... | collective-permute-start | bytes 3145736 | tf_op jit(solution)/shard_map/ppermute | solution.py:25
  85.0 3.7 %collective-permute-start.33 = (f32[3,128]{1,0:T(4,128)S(1)}, f32[3,128]{1,0:T(4,128)S(1)}, u32[]{:S(2)}, u32[]{:S(2)}) collective-permute-start(f32[3,128]{1,0:T(4,128)S(1)} %get-tuple-element.9), channel_id=1, source_target_pairs={{0,8},{1,9},{2,10},{3,11},{4,12},{5,13},{6,14},{7,15},{8,0},{9,1},... | collective-permute-start | bytes 4616 | tf_op jit(solution)/shard_map/ppermute | solution.py:25
  85.6 3.6 %collective-permute-start.34 = (f32[3,128]{1,0:T(4,128)S(1)}, f32[3,128]{1,0:T(4,128)S(1)}, u32[]{:S(2)}, u32[]{:S(2)}) collective-permute-start(f32[3,128]{1,0:T(4,128)S(1)} %get-tuple-element.10), channel_id=1, source_target_pairs={{0,16},{1,17},{2,18},{3,19},{4,20},{5,21},{6,22},{7,23},{8,24},{9,... | collective-permute-start | bytes 4616 | tf_op jit(solution)/shard_map/ppermute | solution.py:25
  87.2 4.5 %collective-permute-start.35 = (f32[3,128]{1,0:T(4,128)S(1)}, f32[3,128]{1,0:T(4,128)S(1)}, u32[]{:S(2)}, u32[]{:S(2)}) collective-permute-start(f32[3,128]{1,0:T(4,128)S(1)} %get-tuple-element.11), channel_id=1, source_target_pairs={{0,24},{1,25},{2,26},{3,27},{4,28},{5,29},{6,30},{7,31},{8,16},{9,... | collective-permute-start | bytes 4616 | tf_op jit(solution)/shard_map/ppermute | solution.py:25
  91.8 6.2 %collective-permute-start.36 = (f32[3,128]{1,0:T(4,128)S(1)}, f32[3,128]{1,0:T(4,128)S(1)}, u32[]{:S(2)}, u32[]{:S(2)}) collective-permute-start(f32[3,128]{1,0:T(4,128)S(1)} %pad_maximum_fusion.6), channel_id=1, source_target_pairs={{0,1},{1,0},{2,3},{3,2},{4,5},{5,4},{6,7},{7,6},{8,9},{9,8},{10,11... | collective-permute-start | bytes 4616 | tf_op jit(solution)/shard_map/ppermute | solution.py:25
  91.8 8.8 %collective-permute-start.37 = (f32[3,128]{1,0:T(4,128)S(1)}, f32[3,128]{1,0:T(4,128)S(1)}, u32[]{:S(2)}, u32[]{:S(2)}) collective-permute-start(f32[3,128]{1,0:T(4,128)S(1)} %pad_maximum_fusion.6), channel_id=1, source_target_pairs={{0,2},{1,3},{2,4},{3,5},{4,6},{5,7},{6,0},{7,1},{8,10},{9,11},{10,... | collective-permute-start | bytes 4616 | tf_op jit(solution)/shard_map/ppermute | solution.py:25
  93.7 8.8 %collective-permute-start.38 = (f32[3,128]{1,0:T(4,128)S(1)}, f32[3,128]{1,0:T(4,128)S(1)}, u32[]{:S(2)}, u32[]{:S(2)}) collective-permute-start(f32[3,128]{1,0:T(4,128)S(1)} %pad_maximum_fusion.6), channel_id=1, source_target_pairs={{0,3},{1,2},{2,5},{3,4},{4,7},{5,6},{6,1},{7,0},{8,11},{9,10},{10,... | collective-permute-start | bytes 4616 | tf_op jit(solution)/shard_map/ppermute | solution.py:25
  93.8 8.7 %collective-permute-start.39 = (f32[3,128]{1,0:T(4,128)S(1)}, f32[3,128]{1,0:T(4,128)S(1)}, u32[]{:S(2)}, u32[]{:S(2)}) collective-permute-start(f32[3,128]{1,0:T(4,128)S(1)} %pad_maximum_fusion.6), channel_id=1, source_target_pairs={{0,4},{1,5},{2,6},{3,7},{4,0},{5,1},{6,2},{7,3},{8,12},{9,13},{10,... | collective-permute-start | bytes 4616 | tf_op jit(solution)/shard_map/ppermute | solution.py:25
  98.0 4.5 %collective-permute-start.40 = (f32[3,128]{1,0:T(4,128)S(1)}, f32[3,128]{1,0:T(4,128)S(1)}, u32[]{:S(2)}, u32[]{:S(2)}) collective-permute-start(f32[3,128]{1,0:T(4,128)S(1)} %pad_maximum_fusion.6), channel_id=1, source_target_pairs={{0,5},{1,4},{2,7},{3,6},{4,1},{5,0},{6,3},{7,2},{8,13},{9,12},{10,... | collective-permute-start | bytes 4616 | tf_op jit(solution)/shard_map/ppermute | solution.py:25
  98.0 4.5 %collective-permute-start.41 = (f32[3,128]{1,0:T(4,128)S(1)}, f32[3,128]{1,0:T(4,128)S(1)}, u32[]{:S(2)}, u32[]{:S(2)}) collective-permute-start(f32[3,128]{1,0:T(4,128)S(1)} %pad_maximum_fusion.6), channel_id=1, source_target_pairs={{0,6},{1,7},{2,0},{3,1},{4,2},{5,3},{6,4},{7,5},{8,14},{9,15},{10,... | collective-permute-start | bytes 4616 | tf_op jit(solution)/shard_map/ppermute | solution.py:25
  100.6 3.0 %collective-permute-start.42 = (f32[3,128]{1,0:T(4,128)S(1)}, f32[3,128]{1,0:T(4,128)S(1)}, u32[]{:S(2)}, u32[]{:S(2)}) collective-permute-start(f32[3,128]{1,0:T(4,128)S(1)} %pad_maximum_fusion.6), channel_id=1, source_target_pairs={{0,7},{1,6},{2,1},{3,0},{4,3},{5,2},{6,5},{7,4},{8,15},{9,14},{10,... | collective-permute-start | bytes 4616 | tf_op jit(solution)/shard_map/ppermute | solution.py:25
  (16 other events, 229.5 us)
